TPU v7x, 32 devices: a whole 2x2x4 slice. The times are simulated.
32 devices in a mesh: grp: 2 (over x), seq: 8 (over z, y), ch: 2 (over core).
Axes of the slice: x: 2, y: 2, z: 4, core: 2. Of those that a mesh axis runs over, the one named last changes fastest.
Arguments:
- q_proj: float32 [2048, 2048], P(('grp', 'seq'), 'ch'), parts along dimension 0, may hold values from -6 to 6
- k_proj: float32 [2048, 2048], P(('grp', 'seq'), 'ch'), parts along dimension 0, may hold values from -6 to 6
- v_proj: float32 [2048, 2048], P(('grp', 'seq'), 'ch'), parts along dimension 0, may hold values from -6 to 6
- short_taps: float32 [3, 3, 2048], P(None, None, 'ch'), may hold values from -3 to 3
- frequencies: int32 [16], replicated, may hold values from 1 to 511
- w_first: float32 [33, 64], replicated, may hold values from -1 to 1
- b_first: float32 [64], replicated, may hold values from -3.140625 to 3.140625
- w_second: float32 [64, 64], replicated, may hold values from -0.75 to 0.75
- b_second: float32 [64], replicated, may hold values from -3.140625 to 3.140625
- w_last: float32 [64, 2048], P(None, 'ch'), may hold values from -0.75 to 0.75
- rates: float32 [2048], P('ch'), may hold values from 0.5 to 200
- skip: float32 [2048], P('ch'), may hold values from -4 to 4
Outputs:
- gated: float32 [2048, 2048], P(('grp', 'seq'), 'ch'), parts along dimension 0
There are 2 independent parts, one for each index of `grp`. A program takes and returns all parts, laid end to end along the dimension named above; an argument that names none is the same for every part. Nothing has to cross between parts.
All inputs are finite; a program needn't handle non-finite values.
Results may differ from a plain program's by a relative error of at most 0.0003.
Values sent between devices are 32-bit elements; how exact they have to be, the bound alone decides.
A program may use at most 64 MiB of HBM per device.

v0:
```python
import math

import jax
import jax.numpy as jnp
from jax import lax
from jax.sharding import PartitionSpec as P

HIGH = lax.Precision.HIGHEST
EPS = 1e-06
DECAY_FLOOR = 0.05


def passed_along(array, axis, by):
    size = lax.axis_size(axis)
    pairs = [(i, i + by) for i in range(size) if 0 <= i + by < size]
    return lax.ppermute(array, axis, pairs)


def causal_short(values, tail, taps):
    count = values.shape[0]
    padded = jnp.concatenate([tail, values], axis=0)
    return taps[0] * values + taps[1] * padded[1 : count + 1] + taps[2] * padded[0:count]


def filter_rows(
    positions, length, frequencies, w_first, b_first, w_second, b_second, w_last, rates
):
    product = positions[:, None] * frequencies[None, :] % length
    angle = 2.0 * math.pi / length * product.astype(jnp.float32)
    place = positions.astype(jnp.float32) / length
    features = jnp.concatenate([place[:, None], jnp.cos(angle), jnp.sin(angle)], axis=1)
    hidden = jnp.sin(jnp.dot(features, w_first, precision=HIGH) + b_first)
    hidden = jnp.sin(jnp.dot(hidden, w_second, precision=HIGH) + b_second)
    raw = jnp.dot(hidden, w_last, precision=HIGH)
    return raw * (jnp.exp(-place[:, None] * rates[None, :]) + DECAY_FLOOR)


def index_table(first_index, second_index, period, sign):
    product = first_index[:, None] * second_index[None, :] % period
    angle = 2.0 * math.pi / period * product.astype(jnp.float32)
    return (jnp.cos(angle), sign * jnp.sin(angle))


def phase_table(first, second, period, sign):
    return index_table(
        jnp.arange(first, dtype=jnp.int32), jnp.arange(second, dtype=jnp.int32), period, sign
    )


def complex_mix(table, values, form):
    cos_part, sin_part = table
    real_in, imag_in = values
    real_out = jnp.einsum(form, cos_part, real_in, precision=HIGH) - jnp.einsum(
        form, sin_part, imag_in, precision=HIGH
    )
    imag_out = jnp.einsum(form, cos_part, imag_in, precision=HIGH) + jnp.einsum(
        form, sin_part, real_in, precision=HIGH
    )
    return (real_out, imag_out)


def rotate(values, table):
    real_in, imag_in = values
    cos_part, sin_part = table
    return (real_in * cos_part - imag_in * sin_part, real_in * sin_part + imag_in * cos_part)


def split_length(length):
    return (16, length // 16)


def local_forward(real_in, imag_in):
    count, length, width = real_in.shape
    radix, remain = split_length(length)
    shaped = (
        real_in.reshape(count, radix, remain, width),
        imag_in.reshape(count, radix, remain, width),
    )
    first = complex_mix(phase_table(radix, radix, radix, -1.0), shaped, "kr,brsc->bksc")
    twist_cos, twist_sin = phase_table(radix, remain, length, -1.0)
    turned = rotate(first, (twist_cos[None, :, :, None], twist_sin[None, :, :, None]))
    second = complex_mix(phase_table(remain, remain, remain, -1.0), turned, "ls,bksc->blkc")
    return (second[0].reshape(count, length, width), second[1].reshape(count, length, width))


def local_inverse(real_in, imag_in):
    count, length, width = real_in.shape
    radix, remain = split_length(length)
    shaped = (
        real_in.reshape(count, remain, radix, width),
        imag_in.reshape(count, remain, radix, width),
    )
    first = complex_mix(phase_table(remain, remain, remain, 1.0), shaped, "sl,blkc->bksc")
    twist_cos, twist_sin = phase_table(radix, remain, length, 1.0)
    turned = rotate(first, (twist_cos[None, :, :, None], twist_sin[None, :, :, None]))
    second = complex_mix(phase_table(radix, radix, radix, 1.0), turned, "rk,bksc->brsc")
    return (second[0].reshape(count, length, width), second[1].reshape(count, length, width))


def offset_twist(values, index, parts, period):
    block = values[0].shape[1]
    offsets = index * block + jnp.arange(block, dtype=jnp.int32)
    twist_cos, twist_sin = index_table(
        jnp.arange(2 * parts, dtype=jnp.int32), offsets, period, -1.0
    )
    return rotate(values, (twist_cos[:, :, None], twist_sin[:, :, None]))


def prepare(columns, index, parts, period):
    cos_part, sin_part = phase_table(2 * parts, parts, 2 * parts, -1.0)
    real_out = jnp.einsum("ka,amc->kmc", cos_part, columns, precision=HIGH)
    imag_out = jnp.einsum("ka,amc->kmc", sin_part, columns, precision=HIGH)
    return offset_twist((real_out, imag_out), index, parts, period)


def forward_two(values):
    return local_forward(values[0], values[1])


def local(
    q_proj,
    k_proj,
    v_proj,
    short_taps,
    frequencies,
    w_first,
    b_first,
    w_second,
    b_second,
    w_last,
    rates,
    skip,
):
    tokens, width = q_proj.shape
    parts = lax.axis_size("seq")
    index = lax.axis_index("seq")
    block = tokens // parts
    length = tokens * parts
    period = 2 * length
    tails = passed_along(
        (q_proj[tokens - 2 :], k_proj[tokens - 2 :], v_proj[tokens - 2 :]), "seq", 1
    )
    q_short = causal_short(q_proj, tails[0], short_taps[0])
    k_short = causal_short(k_proj, tails[1], short_taps[1])
    v_short = causal_short(v_proj, tails[2], short_taps[2])
    mixed = k_short * v_short
    set_order = jnp.arange(2 * parts, dtype=jnp.int32)
    owned_freq = 2 * index + jnp.arange(2, dtype=jnp.int32)
    columns = lax.all_to_all(
        mixed.reshape(parts, block, width), "seq", split_axis=0, concat_axis=0, tiled=True
    )
    mixed_spec = prepare(columns, index, parts, period)
    mixed_freq = forward_two(
        (
            lax.all_to_all(mixed_spec[0], "seq", split_axis=0, concat_axis=1, tiled=True),
            lax.all_to_all(mixed_spec[1], "seq", split_axis=0, concat_axis=1, tiled=True),
        )
    )
    group_size = math.gcd(parts, max(1, 2048 // tokens))
    turn_count = parts // group_size

    def step(carry, turn_index):
        real_acc, imag_acc, energy_acc = carry
        row_index = turn_index * (group_size * tokens) + jnp.arange(
            group_size * tokens, dtype=jnp.int32
        )
        values = filter_rows(
            row_index, length, frequencies, w_first, b_first, w_second, b_second, w_last, rates
        )
        values = values.reshape(group_size, tokens, width)
        sources = turn_index * group_size + jnp.arange(group_size, dtype=jnp.int32)
        cos_part, sin_part = index_table(owned_freq, sources, 2 * parts, -1.0)
        real_acc = real_acc + jnp.einsum("kj,jmc->kmc", cos_part, values, precision=HIGH)
        imag_acc = imag_acc + jnp.einsum("kj,jmc->kmc", sin_part, values, precision=HIGH)
        energy_acc = energy_acc + jnp.sum(values * values, axis=(0, 1))
        return ((real_acc, imag_acc, energy_acc), None)

    start = (
        jnp.zeros((2, tokens, width), jnp.float32),
        jnp.zeros((2, tokens, width), jnp.float32),
        jnp.zeros((width,), jnp.float32),
    )
    (real_acc, imag_acc, energy), _ = lax.scan(step, start, jnp.arange(turn_count, dtype=jnp.int32))
    twist_cos, twist_sin = index_table(
        owned_freq, jnp.arange(tokens, dtype=jnp.int32), period, -1.0
    )
    turned = rotate((real_acc, imag_acc), (twist_cos[:, :, None], twist_sin[:, :, None]))
    filt_freq = local_forward(turned[0], turned[1])
    scale = 1.0 / (period * jnp.sqrt(energy + EPS))
    prod_real = (mixed_freq[0] * filt_freq[0] - mixed_freq[1] * filt_freq[1]) * scale
    prod_imag = (mixed_freq[0] * filt_freq[1] + mixed_freq[1] * filt_freq[0]) * scale
    restored = local_inverse(prod_real, prod_imag)
    untwist_cos, untwist_sin = index_table(
        owned_freq, jnp.arange(tokens, dtype=jnp.int32), period, 1.0
    )
    restored = rotate(restored, (untwist_cos[:, :, None], untwist_sin[:, :, None]))
    values = (
        lax.all_to_all(restored[0], "seq", split_axis=1, concat_axis=0, tiled=True),
        lax.all_to_all(restored[1], "seq", split_axis=1, concat_axis=0, tiled=True),
    )
    cos_part, sin_part = index_table(jnp.arange(parts, dtype=jnp.int32), set_order, 2 * parts, 1.0)
    rows_out = jnp.einsum("ak,kmc->amc", cos_part, values[0], precision=HIGH) - jnp.einsum(
        "ak,kmc->amc", sin_part, values[1], precision=HIGH
    )
    conv = lax.all_to_all(rows_out, "seq", split_axis=0, concat_axis=0, tiled=True).reshape(
        tokens, width
    )
    return q_short * (conv + skip * mixed)


def solution(mesh):
    return jax.shard_map(
        local,
        mesh=mesh,
        in_specs=(
            P(("grp", "seq"), "ch"),
            P(("grp", "seq"), "ch"),
            P(("grp", "seq"), "ch"),
            P(None, None, "ch"),
            P(),
            P(),
            P(),
            P(),
            P(),
            P(None, "ch"),
            P("ch"),
            P("ch"),
        ),
        out_specs=P(("grp", "seq"), "ch"),
        check_vma=False,
    )
```

profile of v0, /device:TPU:0, one launch (start us, length us, event | category | flops | bytes accessed | tf_op | source)
XLA Modules:
  0.0 215.7 jit_solution(4776108297157821510)
XLA Ops:
  0.8 4.9 %collective-permute-start.2 = (f32[2,1024]{1,0:T(2,128)S(1)}, f32[2,1024]{1,0:T(2,128)S(1)}, u32[]{:S(2)}, u32[]{:S(2)}) collective-permute-start(f32[2,1024]{1,0:T(2,128)S(1)} %slice.89), channel_id=1, source_target_pairs={{0,2},{2,4},{4,6},{6,8},{8,10},{10,12},{12,14},{1,3},{3,5},{5,7},{... | collective-permute-start | bytes 24584 | tf_op jit(solution)/shard_map/ppermute | solution.py:16
  6.4 3.4 %collective-permute-start.1 = (f32[2,1024]{1,0:T(2,128)S(1)}, f32[2,1024]{1,0:T(2,128)S(1)}, u32[]{:S(2)}, u32[]{:S(2)}) collective-permute-start(f32[2,1024]{1,0:T(2,128)S(1)} %slice.83), channel_id=1, source_target_pairs={{0,2},{2,4},{4,6},{6,8},{8,10},{10,12},{12,14},{1,3},{3,5},{5,7},{... | collective-permute-start | bytes 24584 | tf_op jit(solution)/shard_map/ppermute | solution.py:16
  9.9 1.5 fusion.352
  11.4 3.2 %fusion.54 = f32[128,1024]{1,0:T(8,128)} fusion(f32[2,1024]{1,0:T(2,128)S(1)} %collective-permute-done.2, f32[128,1024]{1,0:T(8,128)} %param.14, f32[2,1024]{1,0:T(2,128)S(1)} %collective-permute-done.1, f32[128,1024]{1,0:T(8,128)} %param.13, f32[1024]{0:T(1024)S(1)} %bitcast.199, f32[1024]{0:T(1024)S(1)} %bitcast.200, f32[1024]{0:T(1024)S(1)} %bitcast.195, ...), kind=kLoop, calls=%fused_computation.93 | loop fusion | flops 1966080 | bytes 1613824 | tf_op jit(solution)/shard_map/mul | solution.py:146
  14.5 6.4 %all-to-all-start = ((f32[8,16,1024]{2,1,0:T(8,128)}), f32[8,16,1024]{2,1,0:T(8,128)S(1)}, u32[]{:S(2)}, u32[]{:S(2)}) async-start(f32[8,16,1024]{2,1,0:T(8,128)} %bitcast.11), calls=%async_computation | async-start | bytes 1048576 | tf_op jit(solution)/shard_map/all_to_all | solution.py:149
  21.1 12.8 %all-to-all-done = f32[8,16,1024]{2,1,0:T(8,128)S(1)} async-done(((f32[8,16,1024]{2,1,0:T(8,128)}), f32[8,16,1024]{2,1,0:T(8,128)S(1)}, u32[]{:S(2)}, u32[]{:S(2)}) %all-to-all-start) | async-done | bytes 524320 | tf_op jit(solution)/shard_map/all_to_all | solution.py:149
  35.3 1.4 multiply_subtract_fusion.3
  36.6 1.6 copy.152
  38.2 4.0 %all-to-all-start.2 = ((f32[16,16,1024]{2,1,0:T(8,128)}), f32[16,16,1024]{2,1,0:T(8,128)S(1)}, u32[]{:S(2)}, u32[]{:S(2)}) async-start(f32[16,16,1024]{2,1,0:T(8,128)} %copy.152), calls=%async_computation.2 | async-start | bytes 2097152 | tf_op jit(solution)/shard_map/all_to_all | solution.py:156
  46.5 4.9 %multiply_reduce_fusion = (f32[1024]{0:T(1024)}, f32[1024,1024]{1,0:T(8,128)S(1)}) fusion(f32[1024]{0:T(1024)S(1)} %copy-done.19, f32[1024]{0:T(1024)S(1)} %multiply_negate_fusion, f32[1024,64]{0,1:T(8,128)S(1)} %fusion.10, f32[64,1024]{1,0:T(8,128)S(1)} %copy-done), kind=kOutput, calls=%fused_computation | convolution fusion | flops 810548224 | bytes 4730880 | tf_op jit(solution)/shard_map/while/body/eval_jaxpr/dot_general | solution.py:34
  51.4 2.0 copy-done.1
  53.4 6.1 %fusion.2 = f32[2,128,1024]{2,0,1:T(2,128)} fusion(f32[8,128,1024]{2,1,0:T(8,128)S(1)} %bitcast.184, s32[2]{0:T(128)S(1)} %iota_add_fusion), kind=kOutput, calls=%fused_computation.4 | convolution fusion | flops 25166048 | bytes 5242888 | tf_op jit(solution)/shard_map/while/body/eval_jaxpr/kj,jmc->kmc/dot_general | solution.py:173
  59.5 1.6 copy.149
  61.1 6.3 %all-to-all-done.2 = f32[16,16,1024]{2,1,0:T(8,128)S(1)} async-done(((f32[16,16,1024]{2,1,0:T(8,128)}), f32[16,16,1024]{2,1,0:T(8,128)S(1)}, u32[]{:S(2)}, u32[]{:S(2)}) %all-to-all-start.2) | async-done | bytes 1048608 | tf_op jit(solution)/shard_map/all_to_all | solution.py:156
  67.4 4.1 %all-to-all-start.1 = ((f32[16,16,1024]{2,1,0:T(8,128)}), f32[16,16,1024]{2,1,0:T(8,128)S(1)}, u32[]{:S(2)}, u32[]{:S(2)}) async-start(f32[16,16,1024]{2,1,0:T(8,128)} %copy.149), calls=%async_computation.1 | async-start | bytes 2097152 | tf_op jit(solution)/shard_map/all_to_all | solution.py:155
  74.6 9.2 %multiply_subtract_fusion.1 = (f32[2,128,1024]{2,0,1:T(2,128)S(1)}, f32[2,128,1024]{2,0,1:T(2,128)S(1)}) fusion(f32[2,128,1024]{2,0,1:T(2,128)} %fusion.2, f32[2,128]{0,1:T(8,128)S(1)} %copy.162, f32[2,128]{0,1:T(8,128)S(1)} %copy.160, f32[8,128,1024]{2,1,0:T(8,128)} %bitcast.185, s32[2]{0:T(128)} %copy-done.15), kind=kOutput, calls=%fused_computation.48 | convolution fusion | flops 26738928 | bytes 7342088 | tf_op jit(solution)/shard_map/while/body/eval_jaxpr/kj,jmc->kmc/dot_general | solution.py:174
  83.8 1.7 fusion.36
  85.5 2.7 %fusion.32 = f32[2,8,1024,16]{2,3,1,0:T(8,128)} fusion(f32[2,16,8,1024]{3,0,2,1:T(2,128)S(1)} %bitcast.182), kind=kOutput, calls=%fused_computation.65 | convolution fusion | flops 50335232 | bytes 2097152 | tf_op jit(solution)/shard_map/kr,brsc->bksc/dot_general | solution.py:56
  88.2 3.0 %fusion.7 = f32[2,16,8,1024]{3,1,2,0:T(8,128)} fusion(f32[2,8,1024,16]{2,3,1,0:T(8,128)S(1)} %fusion.36, f32[2,16,8,1024]{3,0,2,1:T(2,128)S(1)} %bitcast.183), kind=kOutput, calls=%fused_computation.18 | convolution fusion | flops 50597632 | bytes 3145728 | tf_op jit(solution)/shard_map/kr,brsc->bksc/dot_general | solution.py:53
  91.4 1.6 fusion.44
  93.0 3.7 %all-to-all-done.1 = f32[16,16,1024]{2,1,0:T(8,128)S(1)} async-done(((f32[16,16,1024]{2,1,0:T(8,128)}), f32[16,16,1024]{2,1,0:T(8,128)S(1)}, u32[]{:S(2)}, u32[]{:S(2)}) %all-to-all-start.1) | async-done | bytes 1048608 | tf_op jit(solution)/shard_map/all_to_all | solution.py:155
  96.9 1.6 fusion.48
  98.5 1.6 fusion.8
  100.2 1.6 fusion.9
  101.9 2.5 %multiply_add_fusion = (f32[2,16,8,1024]{3,1,2,0:T(8,128)S(1)}, f32[2,16,8,1024]{3,1,2,0:T(8,128)S(1)}, f32[2,16,8,1024]{3,1,2,0:T(8,128)S(1)}, f32[2,16,8,1024]{3,1,2,0:T(8,128)S(1)}) fusion(f32[2,16,8,1024]{3,1,2,0:T(8,128)S(1)} %copy-done.2, f32[16,8]{0,1:T(8,128)S(1)} %copy-done.12, f32[16,8]{0,1:T(8,128)S(1)} %get-tuple-element.76, ...), kind=kOutput, calls=%fused_computation.45 | convolution fusion | flops 53743360 | bytes 9438208 | tf_op jit(solution)/shard_map/kr,brsc->bksc/dot_general | solution.py:56
  104.4 1.6 fusion.26
  106.0 1.8 fusion.30
  107.9 1.7 convolution_add_fusion.2
  109.5 1.6 fusion.42
  111.2 1.6 fusion.38
  112.8 1.7 convolution_subtract_fusion.4
  114.5 1.7 convolution_subtract_fusion.2
  116.2 2.3 %subtract_multiply_fusion = (f32[2,16,1024,8]{2,3,1,0:T(8,128)S(1)}, f32[2,16,1024,8]{2,3,1,0:T(8,128)S(1)}) fusion(f32[2,16,1024,8]{2,3,1,0:T(8,128)S(1)} %convolution_add_fusion.2, f32[2,16,1024,8]{2,3,1,0:T(8,128)S(1)} %convolution_subtract_fusion.4, f32[2,16,1024,8]{2,3,1,0:T(8,128)S(1)} %convolution_subtract_fusion.2, f32[1024]{0:T(1024)S(1)} %copy-done.13, ...), kind=kOutput, calls=%fused_computation.44 | convolution fusion | flops 27526080 | bytes 7344128 | tf_op jit(solution)/shard_map/ls,bksc->blkc/dot_general | solution.py:56
  118.5 1.5 fusion.14
  122.1 1.4 subtract_bitcast_fusion
  123.5 1.6 fusion.20
  125.2 1.7 fusion.24
  126.8 1.7 fusion.4
  129.4 1.7 fusion.5
  132.1 2.1 fusion.13
  134.2 29.3 %all_to_all.76 = f32[2,128,1024]{2,0,1:T(2,128)S(1)} all-to-all(f32[2,128,1024]{2,0,1:T(2,128)S(1)} %get-tuple-element.30), channel_id=1, replica_groups=mesh['grp'=2,'seq'=8,'ch'=2] {'seq'}, dimensions={1} | all-to-all | bytes 2097152 | tf_op jit(solution)/shard_map/all_to_all | solution.py:198
  163.5 3.6 %all-to-all-start.4 = ((f32[2,128,1024]{2,0,1:T(2,128)}), f32[2,128,1024]{2,0,1:T(2,128)S(1)}, u32[]{:S(2)}, u32[]{:S(2)}) async-start(f32[2,128,1024]{2,0,1:T(2,128)} %get-tuple-element.29), calls=%async_computation.4 | async-start | bytes 2097152 | tf_op jit(solution)/shard_map/all_to_all | solution.py:199
  168.6 24.1 %all-to-all-done.4 = f32[2,128,1024]{2,0,1:T(2,128)S(1)} async-done(((f32[2,128,1024]{2,0,1:T(2,128)}), f32[2,128,1024]{2,0,1:T(2,128)S(1)}, u32[]{:S(2)}, u32[]{:S(2)}) %all-to-all-start.4) | async-done | bytes 1048608 | tf_op jit(solution)/shard_map/all_to_all | solution.py:199
  195.3 3.5 %all-to-all-start.5 = ((f32[8,16,1024]{2,1,0:T(8,128)}), f32[8,16,1024]{2,1,0:T(8,128)S(1)}, u32[]{:S(2)}, u32[]{:S(2)}) async-start(f32[8,16,1024]{2,1,0:T(8,128)} %copy.184), calls=%async_computation.5 | async-start | bytes 1048576 | tf_op jit(solution)/shard_map/all_to_all | solution.py:205
  198.8 3.8 %collective-permute-start = (f32[2,1024]{1,0:T(2,128)S(1)}, f32[2,1024]{1,0:T(2,128)S(1)}, u32[]{:S(2)}, u32[]{:S(2)}) collective-permute-start(f32[2,1024]{1,0:T(2,128)S(1)} %slice.77), channel_id=1, source_target_pairs={{0,2},{2,4},{4,6},{6,8},{8,10},{10,12},{12,14},{1,3},{3,5},{5,7},{... | collective-permute-start | bytes 24584 | tf_op jit(solution)/shard_map/ppermute | solution.py:16
  202.7 1.3 collective-permute-done
  204.0 9.4 %all-to-all-done.5 = f32[8,16,1024]{2,1,0:T(8,128)S(1)} async-done(((f32[8,16,1024]{2,1,0:T(8,128)}), f32[8,16,1024]{2,1,0:T(8,128)S(1)}, u32[]{:S(2)}, u32[]{:S(2)}) %all-to-all-start.5) | async-done | bytes 524320 | tf_op jit(solution)/shard_map/all_to_all | solution.py:205
  213.4 2.1 fusion.63
  (77 shorter events, 18.4 us)
Async XLA Ops:
  0.0 46.5 %copy-start = (f32[64,1024]{1,0:T(8,128)S(1)}, f32[64,1024]{1,0:T(8,128)}, u32[]{:S(2)}) copy-start(f32[64,1024]{1,0:T(8,128)} %param.21) | copy-start | bytes 786436
  0.8 10.6 %collective-permute-start.2 = (f32[2,1024]{1,0:T(2,128)S(1)}, f32[2,1024]{1,0:T(2,128)S(1)}, u32[]{:S(2)}, u32[]{:S(2)}) collective-permute-start(f32[2,1024]{1,0:T(2,128)S(1)} %slice.89), channel_id=1, source_target_pairs={{0,2},{2,4},{4,6},{6,8},{8,10},{10,12},{12,14},{1,3},{3,5},{5,7},{... | collective-permute-start | bytes 24584 | tf_op jit(solution)/shard_map/ppermute | solution.py:16
  6.4 4.9 %collective-permute-start.1 = (f32[2,1024]{1,0:T(2,128)S(1)}, f32[2,1024]{1,0:T(2,128)S(1)}, u32[]{:S(2)}, u32[]{:S(2)}) collective-permute-start(f32[2,1024]{1,0:T(2,128)S(1)} %slice.83), channel_id=1, source_target_pairs={{0,2},{2,4},{4,6},{6,8},{8,10},{10,12},{12,14},{1,3},{3,5},{5,7},{... | collective-permute-start | bytes 24584 | tf_op jit(solution)/shard_map/ppermute | solution.py:16
  14.5 19.4 %all-to-all-start = ((f32[8,16,1024]{2,1,0:T(8,128)}), f32[8,16,1024]{2,1,0:T(8,128)S(1)}, u32[]{:S(2)}, u32[]{:S(2)}) async-start(f32[8,16,1024]{2,1,0:T(8,128)} %bitcast.11), calls=%async_computation | async-start | bytes 1048576 | tf_op jit(solution)/shard_map/all_to_all | solution.py:149
  35.2 8.4 %copy-start.16 = (s32[16]{0:T(128)S(1)}, s32[16]{0:T(128)}, u32[]{:S(2)}) copy-start(s32[16]{0:T(128)} %param.16) | copy-start | bytes 196
  35.2 8.7 %copy-start.9 = (f32[33,64]{1,0:T(8,128)S(1)}, f32[33,64]{1,0:T(8,128)}, u32[]{:S(2)}) copy-start(f32[33,64]{1,0:T(8,128)} %param.17) | copy-start | bytes 25348
  35.2 8.7 %copy-start.17 = (f32[64]{0:T(128)S(1)}, f32[64]{0:T(128)}, u32[]{:S(2)}) copy-start(f32[64]{0:T(128)} %param.18) | copy-start | bytes 772
  35.2 10.0 %copy-start.8 = (f32[64,64]{1,0:T(8,128)S(1)}, f32[64,64]{1,0:T(8,128)}, u32[]{:S(2)}) copy-start(f32[64,64]{1,0:T(8,128)} %param.19) | copy-start | bytes 49156
  35.2 10.0 %copy-start.18 = (f32[64]{0:T(128)S(1)}, f32[64]{0:T(128)}, u32[]{:S(2)}) copy-start(f32[64]{0:T(128)} %param.20) | copy-start | bytes 772
  35.2 11.3 %copy-start.19 = (f32[1024]{0:T(1024)S(1)}, f32[1024]{0:T(1024)}, u32[]{:S(2)}) copy-start(f32[1024]{0:T(1024)} %param.22) | copy-start | bytes 12292
  38.2 29.2 %all-to-all-start.2 = ((f32[16,16,1024]{2,1,0:T(8,128)}), f32[16,16,1024]{2,1,0:T(8,128)S(1)}, u32[]{:S(2)}, u32[]{:S(2)}) async-start(f32[16,16,1024]{2,1,0:T(8,128)} %copy.152), calls=%async_computation.2 | async-start | bytes 2097152 | tf_op jit(solution)/shard_map/all_to_all | solution.py:156
  42.3 17.3 %copy-start.15 = (s32[2]{0:T(128)}, s32[2]{0:T(128)S(1)}, u32[]{:S(2)}) copy-start(s32[2]{0:T(128)S(1)} %iota_add_fusion) | copy-start | bytes 28
  51.4 2.0 copy-start.1
  67.4 29.3 %all-to-all-start.1 = ((f32[16,16,1024]{2,1,0:T(8,128)}), f32[16,16,1024]{2,1,0:T(8,128)S(1)}, u32[]{:S(2)}, u32[]{:S(2)}) async-start(f32[16,16,1024]{2,1,0:T(8,128)} %copy.149), calls=%async_computation.1 | async-start | bytes 2097152 | tf_op jit(solution)/shard_map/all_to_all | solution.py:155
  83.8 7.5 %copy-start.3 = (f32[2,128,1024]{2,0,1:T(2,128)}, f32[2,128,1024]{2,0,1:T(2,128)S(1)}, u32[]{:S(2)}) copy-start(f32[2,128,1024]{2,0,1:T(2,128)S(1)} %get-tuple-element.31) | copy-start | bytes 3145732
  96.8 5.0 %copy-start.2 = (f32[2,16,8,1024]{3,1,2,0:T(8,128)S(1)}, f32[2,16,8,1024]{3,1,2,0:T(8,128)}, u32[]{:S(2)}) copy-start(f32[2,16,8,1024]{3,1,2,0:T(8,128)} %fusion.7) | copy-start | bytes 3145732
  96.8 5.0 %copy-start.4 = (f32[2,128,1024]{2,0,1:T(2,128)S(1)}, f32[2,128,1024]{2,0,1:T(2,128)}, u32[]{:S(2)}) copy-start(f32[2,128,1024]{2,0,1:T(2,128)} %copy-done.3) | copy-start | bytes 3145732
  96.9 5.0 %copy-start.5 = (f32[2,8,1024,16]{2,3,1,0:T(8,128)S(1)}, f32[2,8,1024,16]{2,3,1,0:T(8,128)}, u32[]{:S(2)}) copy-start(f32[2,8,1024,16]{2,3,1,0:T(8,128)} %fusion.32) | copy-start | bytes 3145732
  96.9 5.0 %copy-start.12 = (f32[16,8]{0,1:T(8,128)S(1)}, f32[16,8]{0,1:T(8,128)}, u32[]{:S(2)}) copy-start(f32[16,8]{0,1:T(8,128)} %get-tuple-element.75) | copy-start | bytes 1540
  111.2 5.0 %copy-start.13 = (f32[1024]{0:T(1024)S(1)}, f32[1024]{0:T(1024)}, u32[]{:S(2)}) copy-start(f32[1024]{0:T(1024)} %multiply_divide_fusion) | copy-start | bytes 12292
  118.5 3.7 %copy-start.7 = (f32[16,8]{1,0:T(8,128)S(1)}, f32[16,8]{1,0:T(8,128)}, u32[]{:S(2)}) copy-start(f32[16,8]{1,0:T(8,128)} %copy.173) | copy-start | bytes 1540
  163.5 29.2 %all-to-all-start.4 = ((f32[2,128,1024]{2,0,1:T(2,128)}), f32[2,128,1024]{2,0,1:T(2,128)S(1)}, u32[]{:S(2)}, u32[]{:S(2)}) async-start(f32[2,128,1024]{2,0,1:T(2,128)} %get-tuple-element.29), calls=%async_computation.4 | async-start | bytes 2097152 | tf_op jit(solution)/shard_map/all_to_all | solution.py:199
  192.7 6.1 %copy-start.6 = (f32[128,1024]{1,0:T(8,128)S(1)}, f32[128,1024]{1,0:T(8,128)}, u32[]{:S(2)}) copy-start(f32[128,1024]{1,0:T(8,128)} %param.12) | copy-start | bytes 1572868
  192.7 20.7 %copy-start.10 = (f32[1,1,1024]{2,1,0:T(1,128)S(1)}, f32[1,1,1024]{2,1,0:T(1,128)}, u32[]{:S(2)}) copy-start(f32[1,1,1024]{2,1,0:T(1,128)} %get-tuple-element.60) | copy-start | bytes 12292
  192.7 20.7 %copy-start.11 = (f32[1,1,1024]{2,1,0:T(1,128)S(1)}, f32[1,1,1024]{2,1,0:T(1,128)}, u32[]{:S(2)}) copy-start(f32[1,1,1024]{2,1,0:T(1,128)} %get-tuple-element.61) | copy-start | bytes 12292
  192.7 20.7 %copy-start.14 = (f32[1024]{0:T(1024)S(1)}, f32[1024]{0:T(1024)}, u32[]{:S(2)}) copy-start(f32[1024]{0:T(1024)} %param.23) | copy-start | bytes 12292
  195.3 18.1 %all-to-all-start.5 = ((f32[8,16,1024]{2,1,0:T(8,128)}), f32[8,16,1024]{2,1,0:T(8,128)S(1)}, u32[]{:S(2)}, u32[]{:S(2)}) async-start(f32[8,16,1024]{2,1,0:T(8,128)} %copy.184), calls=%async_computation.5 | async-start | bytes 1048576 | tf_op jit(solution)/shard_map/all_to_all | solution.py:205
  198.8 5.2 %collective-permute-start = (f32[2,1024]{1,0:T(2,128)S(1)}, f32[2,1024]{1,0:T(2,128)S(1)}, u32[]{:S(2)}, u32[]{:S(2)}) collective-permute-start(f32[2,1024]{1,0:T(2,128)S(1)} %slice.77), channel_id=1, source_target_pairs={{0,2},{2,4},{4,6},{6,8},{8,10},{10,12},{12,14},{1,3},{3,5},{5,7},{... | collective-permute-start | bytes 24584 | tf_op jit(solution)/shard_map/ppermute | solution.py:16
where the time goes:
time: 220 us; the launch traced here: 216 us
  matrix products  68.9 us (31%)
  waiting for transfers between devices  57.7 us (26%)
  starting transfers between devices  33.7 us (15%)
  blocking collectives  29.3 us (13%)
  local copies, waits for them, and re-layouts  14.9 us (7%)
  other arithmetic  10.4 us (5%)
    all_to_all x1, blocking collectives, local(): lax.all_to_all(restored[0], 'seq', split_axis=1, concat_axis=0, tiled=True)  29.3 us
    all_to_all x1, waiting for transfers between devices, local(): lax.all_to_all(restored[1], 'seq', split_axis=1, concat_axis=0, tiled=True)  24.1 us
    all_to_all x1, waiting for transfers between devices, local(): lax.all_to_all(mixed.reshape(parts, block, width), 'seq', split_axis=0, c...  12.8 us
    ppermute x3, starting transfers between devices, passed_along(): return lax.ppermute(array, axis, pairs)  12.1 us
    dot_general x6, matrix products, complex_mix(): jnp.einsum(form, sin_part, imag_in, precision=HIGH)  11.1 us
    dot_general x6, matrix products, complex_mix(): jnp.einsum(form, sin_part, real_in, precision=HIGH)  10.8 us
    dot_general x6, matrix products, complex_mix(): jnp.einsum(form, cos_part, imag_in, precision=HIGH)  10.7 us
    dot_general x6, matrix products, complex_mix(): jnp.einsum(form, cos_part, real_in, precision=HIGH)  9.53 us
  transfers between devices with their start and end apart: 8, of which 6 were waited for; matrix products, arithmetic and copies ran while one was open for 19% of the time, Pallas kernels for 0%

commit v1 on v0

v1 whole, which is shorter than its diff:
```python
import functools
import math

import jax
import jax.numpy as jnp
import numpy as np
from jax import lax
from jax.experimental import pallas as pl
from jax.experimental.pallas import tpu as pltpu
from jax.sharding import PartitionSpec as P

HIGH = lax.Precision.HIGHEST
EPS = 1e-06
DECAY_FLOOR = 0.05
LANES = 128
EDGE = 8


def transform_tables(block):
    freq = 2 * np.arange(block)[:, None] + 1
    place = np.arange(2 * block)[None, :]
    angle = 2.0 * np.pi / (4 * block) * (freq * place % (4 * block))
    forward = np.concatenate([np.cos(angle), -np.sin(angle)], axis=0)
    late = angle[:, block:].T
    inverse = np.concatenate([np.cos(late), -np.sin(late)], axis=1) / block
    return forward.astype(np.float32), inverse.astype(np.float32)


def small_sine(x):
    turns = jnp.floor(x * (1.0 / math.pi) + 0.5)
    rest = x - turns * 3.140625
    rest = rest - turns * 9.67502593994140625e-4
    rest = rest - turns * 1.509957990978376432e-7
    odd = (turns.astype(jnp.int32) & 1) == 1
    rest = jnp.where(odd, -rest, rest)
    square = rest * rest
    poly = 2.6083159809786593541503e-06
    poly = poly * square - 0.0001981069071916863322258
    poly = poly * square + 0.00833307858556509017944336
    poly = poly * square - 0.166666597127914428710938
    return rest + rest * (square * poly)


def contract_rows(left, right):
    return lax.dot_general(
        left, right, (((0,), (0,)), ((), ())), precision=HIGH,
        preferred_element_type=jnp.float32,
    )


def kernel(
    parts, flat,
    q_ref, k_ref, v_ref, taps_ref, freq_ref, w1_ref, b1_ref, w2_ref, b2_ref,
    w3_ref, rates_ref, skip_ref, fwd_ref, inv_ref,
    out_ref,
    tails, send, recv, back, conv, feat, w1x, hid, w2x, filt, gain, spec, prod,
    tail_sems, main_sems, edge_sems, back_sems,
):
    tokens, cw = send.shape[1], send.shape[2]
    length = tokens * parts
    me = lax.axis_index("seq")
    order = sorted(range(1, parts), key=lambda s: (-min(s, parts - s), s))

    def ahead(s):
        return lax.rem(me + s, parts)

    def behind(s):
        return lax.rem(me + parts - s, parts)

    def cols(ref, d, rows=slice(None)):
        if flat:
            return ref[rows, pl.ds(pl.multiple_of(d * cw, LANES), cw)]
        return ref[d, rows, :]

    def remote(src, dst, sems, s, dest):
        return pltpu.make_async_remote_copy(
            src_ref=src, dst_ref=dst, send_sem=sems.at[0, s], recv_sem=sems.at[1, s],
            device_id={"seq": dest}, device_id_type=pl.DeviceIdType.MESH,
        )

    barrier = pltpu.get_barrier_semaphore()
    for s in order:
        pl.semaphore_signal(
            barrier, inc=1, device_id={"seq": ahead(s)},
            device_id_type=pl.DeviceIdType.MESH,
        )
    pl.semaphore_wait(barrier, parts - 1)

    last = pl.ds(tokens - EDGE, EDGE)
    tail_copies = []
    for j, ref in enumerate((k_ref, v_ref, q_ref)):
        src = ref.at[last, :] if flat else ref.at[:, last, :]
        copy = remote(src, tails.at[j], tail_sems, j, ahead(1))
        copy.start()
        tail_copies.append(copy)

    def short(ref, j, d):
        rows = tokens - EDGE
        x = cols(ref, d)
        taps = cols(taps_ref, d)
        return (
            taps[3 * j : 3 * j + 1] * x[EDGE:]
            + taps[3 * j + 1 : 3 * j + 2] * x[EDGE - 1 : tokens - 1]
            + taps[3 * j + 2 : 3 * j + 3] * x[EDGE - 2 : tokens - 2]
        )

    def short_edge(ref, j, slot, d):
        x = cols(ref, d, slice(0, EDGE))
        before = cols(tails.at[slot], d)
        before = jnp.where(me == 0, jnp.zeros_like(before), before)
        both = jnp.concatenate([before, x], axis=0)
        taps = cols(taps_ref, d)
        return (
            taps[3 * j : 3 * j + 1] * x
            + taps[3 * j + 1 : 3 * j + 2] * both[EDGE - 1 : 2 * EDGE - 1]
            + taps[3 * j + 2 : 3 * j + 3] * both[EDGE - 2 : 2 * EDGE - 2]
        )

    main_rows = pl.ds(EDGE, tokens - EDGE)
    edge_rows = pl.ds(0, EDGE)
    main_copies, edge_copies, back_copies = {}, {}, {}
    for s in order + [0]:
        d = ahead(s)
        send[d, EDGE:, :] = short(k_ref, 1, d) * short(v_ref, 2, d)
        if s:
            copy = remote(
                send.at[d, main_rows, :], recv.at[me, main_rows, :], main_sems, s, d
            )
            copy.start()
            main_copies[s] = copy
    for copy in tail_copies:
        copy.wait()
    for s in order + [0]:
        d = ahead(s)
        send[d, :EDGE, :] = short_edge(k_ref, 1, 0, d) * short_edge(v_ref, 2, 1, d)
        if s:
            copy = remote(
                send.at[d, edge_rows, :], recv.at[me, edge_rows, :], edge_sems, s, d
            )
            copy.start()
            edge_copies[s] = copy

    width = feat.shape[1]
    bands = freq_ref.shape[0]
    row = lax.broadcasted_iota(jnp.int32, (2 * bands, width), 0)
    position = lax.broadcasted_iota(jnp.int32, (2 * bands, width), 1)
    cycles = jnp.zeros((2 * bands, width), jnp.int32)
    for b in range(bands):
        cycles = jnp.where((row == b) | (row == b + bands), freq_ref[b], cycles)
    quarter = jnp.where(row < bands, length // 4, 0)
    phase = (position * cycles + quarter) & (length - 1)
    feat[...] = jnp.zeros_like(feat)
    feat[0 : 2 * bands, :] = small_sine((2.0 * math.pi / length) * phase.astype(jnp.float32))
    feat[2 * bands : 2 * bands + 1, :] = position[0:1].astype(jnp.float32) / length
    feat[2 * bands + 1 : 2 * bands + 2, :] = jnp.ones((1, width), jnp.float32)
    w1x[...] = jnp.zeros_like(w1x)
    w1x[0 : 2 * bands, :] = w1_ref[1 : 2 * bands + 1, :]
    w1x[2 * bands : 2 * bands + 1, :] = w1_ref[0:1, :]
    w1x[2 * bands + 1 : 2 * bands + 2, :] = b1_ref[...]
    hidden_units = w2_ref.shape[0]
    hid[...] = jnp.zeros_like(hid)
    hid[hidden_units : hidden_units + 1, :] = jnp.ones((1, width), jnp.float32)
    hid[0:hidden_units, :] = small_sine(contract_rows(w1x[...], feat[...]))
    w2x[...] = jnp.zeros_like(w2x)
    w2x[0:hidden_units, :] = w2_ref[...]
    w2x[hidden_units : hidden_units + 1, :] = b2_ref[...]
    hid[0:hidden_units, :] = small_sine(contract_rows(w2x[...], hid[...]))

    filt[0:tokens, :] = jnp.zeros((tokens, cw), jnp.float32)
    w_last = cols(w3_ref, me)
    rates = cols(rates_ref, me)

    def filter_block(j, energy):
        start = pl.multiple_of(j * tokens, tokens)
        raw = contract_rows(hid[0:hidden_units, pl.ds(start, tokens)], w_last)
        n = lax.broadcasted_iota(jnp.int32, (tokens, cw), 0) + j * tokens
        place = n.astype(jnp.float32) / length
        values = raw * (jnp.exp(-place * rates) + DECAY_FLOOR)
        filt[pl.ds(pl.multiple_of(start + tokens, tokens), tokens), :] = values
        return energy + jnp.sum(values * values, axis=0, keepdims=True)

    energy = lax.fori_loop(0, parts, filter_block, jnp.zeros((1, cw), jnp.float32))
    scale = 1.0 / jnp.sqrt(energy + EPS)

    @pl.loop(0, parts)
    def _(j):
        window = filt[pl.ds(pl.multiple_of(j * tokens, tokens), 2 * tokens), :]
        gain[j] = scale * jnp.dot(
            fwd_ref[...], window, precision=HIGH, preferred_element_type=jnp.float32
        )
        prod[j] = jnp.zeros((2 * tokens, cw), jnp.float32)

    def absorb(block, i):
        spec[...] = jnp.dot(
            fwd_ref[:, 0:tokens], block, precision=HIGH, preferred_element_type=jnp.float32
        )

        @pl.loop(0, parts - i)
        def _(j):
            x_re, x_im = spec[0:tokens, :], spec[tokens:, :]
            g_re, g_im = gain[j, 0:tokens, :], gain[j, tokens:, :]
            prod[i + j, 0:tokens, :] += x_re * g_re - x_im * g_im
            prod[i + j, tokens:, :] += x_re * g_im + x_im * g_re

    absorb(send[me], me)
    for s in order:
        main_copies[s].wait_recv()
        edge_copies[s].wait_recv()
        absorb(recv[behind(s)], behind(s))

    def restore(m):
        return jnp.dot(
            inv_ref[...], prod[m], precision=HIGH, preferred_element_type=jnp.float32
        )

    for s in order:
        m = ahead(s)
        conv[m] = restore(m)
        copy = remote(conv.at[m], back.at[me], back_sems, s, m)
        copy.start()
        back_copies[s] = copy
    conv[me] = restore(me)

    def gate(result, d):
        q_short = jnp.concatenate(
            [short_edge(q_ref, 0, 2, d), short(q_ref, 0, d)], axis=0
        )
        value = q_short * (result + cols(skip_ref, d) * send[d])
        if flat:
            out_ref[:, pl.ds(pl.multiple_of(d * cw, LANES), cw)] = value
        else:
            out_ref[d] = value

    gate(conv[me], me)
    for s in order:
        back_copies[s].wait_recv()
        gate(back[behind(s)], behind(s))
    for s in order:
        main_copies[s].wait_send()
        edge_copies[s].wait_send()
        back_copies[s].wait_send()


def local(
    q_proj, k_proj, v_proj, short_taps, frequencies, w_first, b_first, w_second,
    b_second, w_last, rates, skip,
):
    tokens, width = q_proj.shape
    parts = lax.axis_size("seq")
    cw = width // parts
    flat = cw % LANES == 0
    length = tokens * parts
    order = w_second.shape[0]
    features = w_first.shape[0]

    def split(array):
        if flat:
            return array
        return array.reshape(array.shape[0], parts, cw).transpose(1, 0, 2)

    forward, inverse = transform_tables(tokens)
    tail_shape = (3, EDGE, width) if flat else (3, parts, EDGE, cw)
    out_shape = (tokens, width) if flat else (parts, tokens, cw)
    f32 = jnp.float32
    feature_rows = (features + 1 + 7) // 8 * 8
    blocks = pltpu.VMEM((parts, tokens, cw), f32)
    spectra = pltpu.VMEM((parts, 2 * tokens, cw), f32)
    vmem = pl.BlockSpec(memory_space=pltpu.VMEM)
    smem = pl.BlockSpec(memory_space=pltpu.SMEM)
    sems = pltpu.SemaphoreType.DMA((2, parts))
    out = pl.pallas_call(
        functools.partial(kernel, parts, flat),
        out_shape=jax.ShapeDtypeStruct(out_shape, f32),
        in_specs=[vmem] * 4 + [smem] + [vmem] * 9,
        out_specs=vmem,
        scratch_shapes=[
            pltpu.VMEM(tail_shape, f32),
            blocks, blocks, blocks, blocks,
            pltpu.VMEM((feature_rows, length), f32),
            pltpu.VMEM((feature_rows, order), f32),
            pltpu.VMEM((order + 8, length), f32),
            pltpu.VMEM((order + 8, order), f32),
            pltpu.VMEM((length + tokens, cw), f32),
            spectra,
            pltpu.VMEM((2 * tokens, cw), f32),
            spectra,
            pltpu.SemaphoreType.DMA((2, 3)),
            sems, sems, sems,
        ],
        compiler_params=pltpu.CompilerParams(
            collective_id=0, has_side_effects=True, vmem_limit_bytes=48 * 1024 * 1024
        ),
        cost_estimate=pl.CostEstimate(
            flops=6 * length * tokens * cw * 8, bytes_accessed=16 * tokens * width,
            transcendentals=length * cw,
        ),
    )(
        split(q_proj), split(k_proj), split(v_proj),
        split(short_taps.reshape(9, width)), frequencies,
        w_first, b_first.reshape(1, order), w_second, b_second.reshape(1, order),
        split(w_last), split(rates.reshape(1, width)), split(skip.reshape(1, width)),
        jnp.asarray(forward), jnp.asarray(inverse),
    )
    if not flat:
        out = out.transpose(1, 0, 2).reshape(tokens, width)
    return out


def solution(mesh):
    return jax.shard_map(
        local,
        mesh=mesh,
        in_specs=(
            P(("grp", "seq"), "ch"),
            P(("grp", "seq"), "ch"),
            P(("grp", "seq"), "ch"),
            P(None, None, "ch"),
            P(),
            P(),
            P(),
            P(),
            P(),
            P(None, "ch"),
            P("ch"),
            P("ch"),
        ),
        out_specs=P(("grp", "seq"), "ch"),
        check_vma=False,
    )
```

time: 220 us -> 44 us (0.20); the launches traced: 216 us -> 43.6 us
  matrix products: 68.9 us -> 0 us
  waiting for transfers between devices: 57.7 us -> 0 us
  Pallas kernels: 0 us -> 35.9 us
  starting transfers between devices: 33.7 us -> 0 us
  blocking collectives: 29.3 us -> 0 us
  other arithmetic: 10.4 us -> 0 us
  local copies, waits for them, and re-layouts: 14.9 us -> 7.64 us
    dot_general x33 -> x0, matrix products: 68.9 us -> none  [the longest x6 11.1 us: complex_mix(): jnp.einsum(form, sin_part, imag_in, precision=HIGH)]
    all_to_all x5 -> x0, waiting for transfers between devices: 56.3 us -> none  [the longest x1 24.1 us: local(): lax.all_to_all(restored[1], 'seq', split_axis=1, concat_axis=0, tiled=True)]
    pallas_call x0 -> x1, Pallas kernels: none -> 35.9 us  [local(): pl.pallas_call(functools.partial(kernel, parts, flat), out_shape=jax.Shap...]
    all_to_all x1 -> x0, blocking collectives: 29.3 us -> none  [local(): lax.all_to_all(restored[0], 'seq', split_axis=1, concat_axis=0, tiled=True)]
    all_to_all x5 -> x0, starting transfers between devices: 21.6 us -> none  [the longest x1 6.37 us: local(): lax.all_to_all(mixed.reshape(parts, block, width), 'seq', split_axis=0, c...]
    ppermute x3 -> x0, starting transfers between devices: 12.1 us -> none  [passed_along(): return lax.ppermute(array, axis, pairs)]
    mul x3 -> x0, other arithmetic: 5.89 us -> none  [the longest x1 3.16 us: local(): mixed = k_short * v_short]
    unnamed x40 -> x27, local copies, waits for them, and re-layouts: 2.08 us -> 6.74 us
  transfers between devices with their start and end apart: 8 -> 0, of which waited for: 6 -> 0; matrix products, arithmetic and copies ran while one was open for 19% -> 0% of each run, Pallas kernels for 0% -> 0%
where the time goes in v1:
time: 44 us; the launch traced here: 43.6 us
  Pallas kernels  35.9 us (82%)
  local copies, waits for them, and re-layouts  7.64 us (17%)
    pallas_call x1, Pallas kernels, local(): pl.pallas_call(functools.partial(kernel, parts, flat), out_shape=jax.Shap...  35.9 us
    unnamed x27, local copies, waits for them, and re-layouts  6.74 us
    reshape x1, local copies, waits for them, and re-layouts, local(): short_taps.reshape(9, width)  0.89 us

profile of v1, /device:TPU:0, one launch (start us, length us, event | category | flops | bytes accessed | tf_op | source)
XLA Modules:
  0.0 43.6 jit_solution(1774328446552305182)
XLA Ops:
  0.0 0.0 copy-start.4
  0.0 0.0 copy-start.5
  0.0 0.0 copy-start.6
  0.0 0.0 copy-start.7
  0.0 0.0 copy-start.8
  0.0 0.0 copy-start.9
  0.0 0.0 copy-start.10
  0.0 0.9 %reshape.15.taps_ref = f32[9,1024]{1,0:T(8,128)S(1)} reshape(f32[3,3,1024]{2,1,0:T(4,128)} %param.17) | data formatting | bytes 73728 | tf_op jit(solution)/shard_map/reshape | solution.py:299
  0.9 0.0 copy-done.4
  0.9 0.0 copy-done.5
  1.0 0.0 copy-done.6
  1.0 0.0 copy-done.7
  1.0 0.0 copy-done.8
  1.0 0.0 copy-done.9
  1.0 0.0 copy-done.10
  1.0 0.0 copy-start
  1.0 1.0 %copy-done = f32[128,1024]{1,0:T(8,128)S(1)} copy-done((f32[128,1024]{1,0:T(8,128)S(1)}, f32[128,1024]{1,0:T(8,128)}, u32[]{:S(2)}) %copy-start) | copy-done | bytes 524312
  2.0 0.0 copy-start.1
  2.0 1.0 %copy-done.1 = f32[128,1024]{1,0:T(8,128)S(1)} copy-done((f32[128,1024]{1,0:T(8,128)S(1)}, f32[128,1024]{1,0:T(8,128)}, u32[]{:S(2)}) %copy-start.1) | copy-done | bytes 524312
  3.1 0.0 copy-start.2
  3.1 1.0 %copy-done.2 = f32[128,1024]{1,0:T(8,128)S(1)} copy-done((f32[128,1024]{1,0:T(8,128)S(1)}, f32[128,1024]{1,0:T(8,128)}, u32[]{:S(2)}) %copy-start.2) | copy-done | bytes 524312
  4.1 0.0 copy-start.3
  4.1 0.9 %copy-done.3 = f32[64,1024]{1,0:T(8,128)S(1)} copy-done((f32[64,1024]{1,0:T(8,128)S(1)}, f32[64,1024]{1,0:T(8,128)}, u32[]{:S(2)}) %copy-start.3) | copy-done | bytes 262168
  5.1 0.0 copy-start.11
  5.1 0.9 %copy-done.11 = f32[256,256]{1,0:T(8,128)S(1)} copy-done((f32[256,256]{1,0:T(8,128)S(1)}, f32[256,256]{1,0:T(8,128)}, u32[]{:S(2)}) %copy-start.11) | copy-done | bytes 262168
  6.0 0.0 copy-start.12
  6.0 0.9 %copy-done.12 = f32[128,256]{1,0:T(8,128)S(1)} copy-done((f32[128,256]{1,0:T(8,128)S(1)}, f32[128,256]{1,0:T(8,128)}, u32[]{:S(2)}) %copy-start.12) | copy-done | bytes 131096
  6.9 35.9 %shard_map.136 = f32[128,1024]{1,0:T(8,128)S(1)} custom-call(f32[128,1024]{1,0:T(8,128)S(1)} %copy-done, f32[128,1024]{1,0:T(8,128)S(1)} %copy-done.1, f32[128,1024]{1,0:T(8,128)S(1)} %copy-done.2, f32[9,1024]{1,0:T(8,128)S(1)} %reshape.15.taps_ref, s32[16]{0:T(128)S(1)} %copy-done.8, f32[33,64]{1,0:T(8,128)S(1)} %copy-done.5, f32[1,64]{1,0:T(1,128)S(1)} %bitcast.6, ...), custom_call_target="tpu_custom_call" | custom-call | flops 805306368 | bytes 2097152 | tf_op jit(solution)/shard_map/pallas_call | solution.py:271
  42.8 0.8 %copy.16 = f32[128,1024]{1,0:T(8,128)} copy(f32[128,1024]{1,0:T(8,128)S(1)} %shard_map.136) | data formatting | bytes 1048576
Async XLA Ops:
  0.0 0.9 %copy-start.4 = (f32[64,64]{1,0:T(8,128)S(1)}, f32[64,64]{1,0:T(8,128)}, u32[]{:S(2)}) copy-start(f32[64,64]{1,0:T(8,128)} %w2_ref.1) | copy-start | bytes 49156
  0.0 0.9 %copy-start.5 = (f32[33,64]{1,0:T(8,128)S(1)}, f32[33,64]{1,0:T(8,128)}, u32[]{:S(2)}) copy-start(f32[33,64]{1,0:T(8,128)} %w1_ref.1) | copy-start | bytes 25348
  0.0 0.9 %copy-start.6 = (f32[1024]{0:T(1024)S(1)}, f32[1024]{0:T(1024)}, u32[]{:S(2)}) copy-start(f32[1024]{0:T(1024)} %param.24) | copy-start | bytes 12292
  0.0 1.0 %copy-start.7 = (f32[1024]{0:T(1024)S(1)}, f32[1024]{0:T(1024)}, u32[]{:S(2)}) copy-start(f32[1024]{0:T(1024)} %param.25) | copy-start | bytes 12292
  0.0 1.0 %copy-start.8 = (s32[16]{0:T(128)S(1)}, s32[16]{0:T(128)}, u32[]{:S(2)}) copy-start(s32[16]{0:T(128)} %freq_ref.1) | copy-start | bytes 196
  0.0 1.0 %copy-start.9 = (f32[64]{0:T(128)S(1)}, f32[64]{0:T(128)}, u32[]{:S(2)}) copy-start(f32[64]{0:T(128)} %param.20) | copy-start | bytes 772
  0.0 1.0 %copy-start.10 = (f32[64]{0:T(128)S(1)}, f32[64]{0:T(128)}, u32[]{:S(2)}) copy-start(f32[64]{0:T(128)} %param.22) | copy-start | bytes 772
  1.0 1.0 %copy-start = (f32[128,1024]{1,0:T(8,128)S(1)}, f32[128,1024]{1,0:T(8,128)}, u32[]{:S(2)}) copy-start(f32[128,1024]{1,0:T(8,128)} %q_ref.1) | copy-start | bytes 1572868
  2.0 1.0 %copy-start.1 = (f32[128,1024]{1,0:T(8,128)S(1)}, f32[128,1024]{1,0:T(8,128)}, u32[]{:S(2)}) copy-start(f32[128,1024]{1,0:T(8,128)} %k_ref.1) | copy-start | bytes 1572868
  3.1 1.0 %copy-start.2 = (f32[128,1024]{1,0:T(8,128)S(1)}, f32[128,1024]{1,0:T(8,128)}, u32[]{:S(2)}) copy-start(f32[128,1024]{1,0:T(8,128)} %v_ref.1) | copy-start | bytes 1572868
  4.1 0.9 %copy-start.3 = (f32[64,1024]{1,0:T(8,128)S(1)}, f32[64,1024]{1,0:T(8,128)}, u32[]{:S(2)}) copy-start(f32[64,1024]{1,0:T(8,128)} %w3_ref.1) | copy-start | bytes 786436
  5.1 0.9 %copy-start.11 = (f32[256,256]{1,0:T(8,128)S(1)}, f32[256,256]{1,0:T(8,128)}, u32[]{:S(2)}) copy-start(f32[256,256]{1,0:T(8,128)} %constant.4.clone.fwd_ref) | copy-start | bytes 786436
  6.0 0.9 %copy-start.12 = (f32[128,256]{1,0:T(8,128)S(1)}, f32[128,256]{1,0:T(8,128)}, u32[]{:S(2)}) copy-start(f32[128,256]{1,0:T(8,128)} %constant.5.clone.inv_ref) | copy-start | bytes 393220

commit v2 on v1

--- a/solution.py
+++ b/solution.py
@@ -50,9 +50,11 @@
 
 def kernel(
     parts, flat,
-    q_ref, k_ref, v_ref, taps_ref, freq_ref, w1_ref, b1_ref, w2_ref, b2_ref,
-    w3_ref, rates_ref, skip_ref, fwd_ref, inv_ref,
+    q_hbm, k_hbm, v_hbm, taps_hbm, freq_ref, w1_hbm, b1_hbm, w2_hbm, b2_hbm,
+    w3_hbm, rates_hbm, skip_hbm, fwd_hbm, inv_hbm,
     out_ref,
+    q_ref, k_ref, v_ref, taps_ref, w1_ref, b1_ref, w2_ref, b2_ref, w3_ref, rates_ref,
+    skip_ref, fwd_ref, inv_ref, load_sems, block_sems,
     tails, send, recv, back, conv, feat, w1x, hid, w2x, filt, gain, spec, prod,
     tail_sems, main_sems, edge_sems, back_sems,
 ):
@@ -72,6 +74,35 @@
             return ref[rows, pl.ds(pl.multiple_of(d * cw, LANES), cw)]
         return ref[d, rows, :]
 
+    def part_of(ref, d):
+        if flat:
+            return ref.at[:, pl.ds(pl.multiple_of(d * cw, LANES), cw)]
+        return ref.at[d]
+
+    def taps_of(j, d):
+        if flat:
+            return taps_ref[j, :, pl.ds(pl.multiple_of(d * cw, LANES), cw)]
+        return taps_ref[d, j]
+
+    block_loads = {}
+    small = {}
+
+    def load(name, src, dst):
+        small[name] = pltpu.make_async_copy(src, dst, load_sems.at[len(small)])
+        small[name].start()
+
+    def load_block(j, src, dst, s):
+        d = ahead(s)
+        block_loads[j, s] = pltpu.make_async_copy(
+            part_of(src, d), dst.at[d], block_sems.at[j, s]
+        )
+        block_loads[j, s].start()
+
+    load("taps", taps_hbm, taps_ref)
+    for s in order + [0]:
+        load_block(1, k_hbm, k_ref, s)
+        load_block(2, v_hbm, v_ref, s)
+
     def remote(src, dst, sems, s, dest):
         return pltpu.make_async_remote_copy(
             src_ref=src, dst_ref=dst, send_sem=sems.at[0, s], recv_sem=sems.at[1, s],
@@ -88,39 +119,52 @@
 
     last = pl.ds(tokens - EDGE, EDGE)
     tail_copies = []
-    for j, ref in enumerate((k_ref, v_ref, q_ref)):
+    for j, ref in enumerate((k_hbm, v_hbm, q_hbm)):
         src = ref.at[last, :] if flat else ref.at[:, last, :]
         copy = remote(src, tails.at[j], tail_sems, j, ahead(1))
         copy.start()
         tail_copies.append(copy)
+    load("w1", w1_hbm, w1_ref)
+    load("b1", b1_hbm, b1_ref)
+    load("w2", w2_hbm, w2_ref)
+    load("b2", b2_hbm, b2_ref)
+    load("w3", part_of(w3_hbm, me), w3_ref)
+    load("rates", part_of(rates_hbm, me), rates_ref)
+    load("fwd", fwd_hbm, fwd_ref)
+    load("inv", inv_hbm, inv_ref)
+    load("skip", skip_hbm, skip_ref)
+    for s in order + [0]:
+        load_block(0, q_hbm, q_ref, s)
 
     def short(ref, j, d):
-        rows = tokens - EDGE
-        x = cols(ref, d)
-        taps = cols(taps_ref, d)
+        x = ref[d]
+        taps = taps_of(j, d)
         return (
-            taps[3 * j : 3 * j + 1] * x[EDGE:]
-            + taps[3 * j + 1 : 3 * j + 2] * x[EDGE - 1 : tokens - 1]
-            + taps[3 * j + 2 : 3 * j + 3] * x[EDGE - 2 : tokens - 2]
+            taps[0:1] * x[EDGE:]
+            + taps[1:2] * x[EDGE - 1 : tokens - 1]
+            + taps[2:3] * x[EDGE - 2 : tokens - 2]
         )
 
     def short_edge(ref, j, slot, d):
-        x = cols(ref, d, slice(0, EDGE))
+        x = ref[d, 0:EDGE, :]
         before = cols(tails.at[slot], d)
         before = jnp.where(me == 0, jnp.zeros_like(before), before)
         both = jnp.concatenate([before, x], axis=0)
-        taps = cols(taps_ref, d)
+        taps = taps_of(j, d)
         return (
-            taps[3 * j : 3 * j + 1] * x
-            + taps[3 * j + 1 : 3 * j + 2] * both[EDGE - 1 : 2 * EDGE - 1]
-            + taps[3 * j + 2 : 3 * j + 3] * both[EDGE - 2 : 2 * EDGE - 2]
+            taps[0:1] * x
+            + taps[1:2] * both[EDGE - 1 : 2 * EDGE - 1]
+            + taps[2:3] * both[EDGE - 2 : 2 * EDGE - 2]
         )
 
     main_rows = pl.ds(EDGE, tokens - EDGE)
     edge_rows = pl.ds(0, EDGE)
     main_copies, edge_copies, back_copies = {}, {}, {}
+    small["taps"].wait()
     for s in order + [0]:
         d = ahead(s)
+        block_loads[1, s].wait()
+        block_loads[2, s].wait()
         send[d, EDGE:, :] = short(k_ref, 1, d) * short(v_ref, 2, d)
         if s:
             copy = remote(
@@ -140,6 +184,8 @@
             copy.start()
             edge_copies[s] = copy
 
+    for name in ("w1", "b1", "w2", "b2", "w3", "rates", "fwd", "inv", "skip"):
+        small[name].wait()
     width = feat.shape[1]
     bands = freq_ref.shape[0]
     row = lax.broadcasted_iota(jnp.int32, (2 * bands, width), 0)
@@ -167,8 +213,8 @@
     hid[0:hidden_units, :] = small_sine(contract_rows(w2x[...], hid[...]))
 
     filt[0:tokens, :] = jnp.zeros((tokens, cw), jnp.float32)
-    w_last = cols(w3_ref, me)
-    rates = cols(rates_ref, me)
+    w_last = w3_ref[...]
+    rates = rates_ref[...]
 
     def filter_block(j, energy):
         start = pl.multiple_of(j * tokens, tokens)
@@ -231,6 +277,8 @@
         else:
             out_ref[d] = value
 
+    for s in order + [0]:
+        block_loads[0, s].wait()
     gate(conv[me], me)
     for s in order:
         back_copies[s].wait_recv()
@@ -266,14 +314,31 @@
     blocks = pltpu.VMEM((parts, tokens, cw), f32)
     spectra = pltpu.VMEM((parts, 2 * tokens, cw), f32)
     vmem = pl.BlockSpec(memory_space=pltpu.VMEM)
+    hbm = pl.BlockSpec(memory_space=pltpu.HBM)
     smem = pl.BlockSpec(memory_space=pltpu.SMEM)
     sems = pltpu.SemaphoreType.DMA((2, parts))
+    taps = short_taps
+    if not flat:
+        taps = taps.reshape(3, 3, parts, cw).transpose(2, 0, 1, 3)
     out = pl.pallas_call(
         functools.partial(kernel, parts, flat),
         out_shape=jax.ShapeDtypeStruct(out_shape, f32),
-        in_specs=[vmem] * 4 + [smem] + [vmem] * 9,
+        in_specs=[hbm] * 4 + [smem] + [hbm] * 9,
         out_specs=vmem,
         scratch_shapes=[
+            blocks, blocks, blocks,
+            pltpu.VMEM(taps.shape, f32),
+            pltpu.VMEM((features, order), f32),
+            pltpu.VMEM((1, order), f32),
+            pltpu.VMEM((order, order), f32),
+            pltpu.VMEM((1, order), f32),
+            pltpu.VMEM((order, cw), f32),
+            pltpu.VMEM((1, cw), f32),
+            pltpu.VMEM((1, width) if flat else (parts, 1, cw), f32),
+            pltpu.VMEM((2 * tokens, 2 * tokens), f32),
+            pltpu.VMEM((tokens, 2 * tokens), f32),
+            pltpu.SemaphoreType.DMA((10,)),
+            pltpu.SemaphoreType.DMA((3, parts)),
             pltpu.VMEM(tail_shape, f32),
             blocks, blocks, blocks, blocks,
             pltpu.VMEM((feature_rows, length), f32),
@@ -288,7 +353,7 @@
             sems, sems, sems,
         ],
         compiler_params=pltpu.CompilerParams(
-            collective_id=0, has_side_effects=True, vmem_limit_bytes=48 * 1024 * 1024
+            collective_id=0, has_side_effects=True, vmem_limit_bytes=62 * 1024 * 1024
         ),
         cost_estimate=pl.CostEstimate(
             flops=6 * length * tokens * cw * 8, bytes_accessed=16 * tokens * width,
@@ -296,7 +361,7 @@
         ),
     )(
         split(q_proj), split(k_proj), split(v_proj),
-        split(short_taps.reshape(9, width)), frequencies,
+        taps, frequencies,
         w_first, b_first.reshape(1, order), w_second, b_second.reshape(1, order),
         split(w_last), split(rates.reshape(1, width)), split(skip.reshape(1, width)),
         jnp.asarray(forward), jnp.asarray(inverse),

time: 44 us -> 38.9 us (0.88)
  local copies, waits for them, and re-layouts: 7.64 us -> 1.89 us
  Pallas kernels: 35.9 us -> 36.9 us
    unnamed x27 -> x1, local copies, waits for them, and re-layouts: 6.74 us -> 1.89 us
    pallas_call x1, Pallas kernels: 35.9 us -> 36.9 us  [local(): pl.pallas_call(functools.partial(kernel, parts, flat), out_shape=jax.Shap...]
    reshape x1 -> x0, local copies, waits for them, and re-layouts: 0.89 us -> none  [local(): short_taps.reshape(9, width)]
where the time goes in v2:
time: 38.9 us; the launch traced here: 38.8 us
  Pallas kernels  36.9 us (95%)
  local copies, waits for them, and re-layouts  1.89 us (5%)
    pallas_call x1, Pallas kernels, local(): pl.pallas_call(functools.partial(kernel, parts, flat), out_shape=jax.Shap...  36.9 us
    unnamed x1, local copies, waits for them, and re-layouts  1.89 us

profile of v2, /device:TPU:0, one launch (start us, length us, event | category | flops | bytes accessed | tf_op | source)
XLA Modules:
  0.0 38.8 jit_solution(11539215584791284128)
XLA Ops:
  0.0 36.9 %shard_map.136 = f32[128,1024]{1,0:T(8,128)} custom-call(f32[128,1024]{1,0:T(8,128)} %q_hbm.1, f32[128,1024]{1,0:T(8,128)} %k_hbm.1, f32[128,1024]{1,0:T(8,128)} %v_hbm.1, f32[3,3,1024]{2,1,0:T(4,128)} %taps_hbm.1, s32[16]{0:T(128)} %freq_ref.1, f32[33,64]{1,0:T(8,128)} %w1_hbm.1, f32[1,64]{1,0:T(1,128)} %bitcast.6, f32[64,64]{1,0:T(8,128)} %w2_hbm.1, ...), custom_call_target="tpu_custom_call" | custom-call | flops 805306368 | bytes 2097152 | tf_op jit(solution)/shard_map/pallas_call | solution.py:323
  36.9 1.9 %copy.16 = f32[128,1024]{1,0:T(8,128)} copy(f32[128,1024]{1,0:T(8,128)} %shard_map.136) | data formatting | bytes 1048576

commit v3 on v2

--- a/solution.py
+++ b/solution.py
@@ -61,7 +61,10 @@
     tokens, cw = send.shape[1], send.shape[2]
     length = tokens * parts
     me = lax.axis_index("seq")
-    order = sorted(range(1, parts), key=lambda s: (-min(s, parts - s), s))
+    half = parts // 2
+
+    def turn(t):
+        return half + (1 - 2 * (t % 2)) * ((t + 1) // 2)
 
     def ahead(s):
         return lax.rem(me + s, parts)
@@ -84,24 +87,31 @@
             return taps_ref[j, :, pl.ds(pl.multiple_of(d * cw, LANES), cw)]
         return taps_ref[d, j]
 
-    block_loads = {}
+    barrier = pltpu.get_barrier_semaphore()
+
+    @pl.loop(1, parts)
+    def _(s):
+        pl.semaphore_signal(
+            barrier, inc=1, device_id={"seq": ahead(s)},
+            device_id_type=pl.DeviceIdType.MESH,
+        )
+
     small = {}
 
     def load(name, src, dst):
         small[name] = pltpu.make_async_copy(src, dst, load_sems.at[len(small)])
         small[name].start()
 
-    def load_block(j, src, dst, s):
+    def block_load(j, src, dst, s):
         d = ahead(s)
-        block_loads[j, s] = pltpu.make_async_copy(
-            part_of(src, d), dst.at[d], block_sems.at[j, s]
-        )
-        block_loads[j, s].start()
+        return pltpu.make_async_copy(part_of(src, d), dst.at[d], block_sems.at[j, s])
 
     load("taps", taps_hbm, taps_ref)
-    for s in order + [0]:
-        load_block(1, k_hbm, k_ref, s)
-        load_block(2, v_hbm, v_ref, s)
+
+    @pl.loop(0, parts)
+    def _(t):
+        block_load(1, k_hbm, k_ref, turn(t)).start()
+        block_load(2, v_hbm, v_ref, turn(t)).start()
 
     def remote(src, dst, sems, s, dest):
         return pltpu.make_async_remote_copy(
@@ -109,21 +119,7 @@
             device_id={"seq": dest}, device_id_type=pl.DeviceIdType.MESH,
         )
 
-    barrier = pltpu.get_barrier_semaphore()
-    for s in order:
-        pl.semaphore_signal(
-            barrier, inc=1, device_id={"seq": ahead(s)},
-            device_id_type=pl.DeviceIdType.MESH,
-        )
-    pl.semaphore_wait(barrier, parts - 1)
-
-    last = pl.ds(tokens - EDGE, EDGE)
-    tail_copies = []
-    for j, ref in enumerate((k_hbm, v_hbm, q_hbm)):
-        src = ref.at[last, :] if flat else ref.at[:, last, :]
-        copy = remote(src, tails.at[j], tail_sems, j, ahead(1))
-        copy.start()
-        tail_copies.append(copy)
+
     load("w1", w1_hbm, w1_ref)
     load("b1", b1_hbm, b1_ref)
     load("w2", w2_hbm, w2_ref)
@@ -133,8 +129,10 @@
     load("fwd", fwd_hbm, fwd_ref)
     load("inv", inv_hbm, inv_ref)
     load("skip", skip_hbm, skip_ref)
-    for s in order + [0]:
-        load_block(0, q_hbm, q_ref, s)
+
+    @pl.loop(0, parts)
+    def _(t):
+        block_load(0, q_hbm, q_ref, turn(t)).start()
 
     def short(ref, j, d):
         x = ref[d]
@@ -159,30 +157,62 @@
 
     main_rows = pl.ds(EDGE, tokens - EDGE)
     edge_rows = pl.ds(0, EDGE)
-    main_copies, edge_copies, back_copies = {}, {}, {}
+    def main_copy(s):
+        d = ahead(s)
+        return remote(
+            send.at[d, main_rows, :], recv.at[me, main_rows, :], main_sems, s, d
+        )
+
+    def edge_copy(s):
+        d = ahead(s)
+        return remote(
+            send.at[d, edge_rows, :], recv.at[me, edge_rows, :], edge_sems, s, d
+        )
+
+    def back_copy(s):
+        m = ahead(s)
+        return remote(conv.at[m], back.at[me], back_sems, s, m)
+
     small["taps"].wait()
-    for s in order + [0]:
+
+    def mix_main(s):
         d = ahead(s)
-        block_loads[1, s].wait()
-        block_loads[2, s].wait()
+        block_load(1, k_hbm, k_ref, s).wait()
+        block_load(2, v_hbm, v_ref, s).wait()
         send[d, EDGE:, :] = short(k_ref, 1, d) * short(v_ref, 2, d)
-        if s:
-            copy = remote(
-                send.at[d, main_rows, :], recv.at[me, main_rows, :], main_sems, s, d
-            )
-            copy.start()
-            main_copies[s] = copy
+
+    def mix_edge(s):
+        d = ahead(s)
+        send[d, :EDGE, :] = short_edge(k_ref, 1, 0, d) * short_edge(v_ref, 2, 1, d)
+
+    @pl.loop(0, parts)
+    def _(t):
+        mix_main(turn(t))
+
+    pl.semaphore_wait(barrier, parts - 1)
+
+    last = pl.ds(tokens - EDGE, EDGE)
+    tail_copies = []
+    for j, ref in enumerate((k_hbm, v_hbm, q_hbm)):
+        src = ref.at[last, :] if flat else ref.at[:, last, :]
+        copy = remote(src, tails.at[j], tail_sems, j, ahead(1))
+        copy.start()
+        tail_copies.append(copy)
+    @pl.loop(0, parts - 1)
+    def _(t):
+        main_copy(turn(t)).start()
+
     for copy in tail_copies:
         copy.wait()
-    for s in order + [0]:
-        d = ahead(s)
-        send[d, :EDGE, :] = short_edge(k_ref, 1, 0, d) * short_edge(v_ref, 2, 1, d)
-        if s:
-            copy = remote(
-                send.at[d, edge_rows, :], recv.at[me, edge_rows, :], edge_sems, s, d
-            )
-            copy.start()
-            edge_copies[s] = copy
+
+    @pl.loop(0, parts)
+    def _(t):
+        s = turn(t)
+        mix_edge(s)
+
+        @pl.when(t < parts - 1)
+        def _():
+            edge_copy(s).start()
 
     for name in ("w1", "b1", "w2", "b2", "w3", "rates", "fwd", "inv", "skip"):
         small[name].wait()
@@ -249,9 +279,12 @@
             prod[i + j, tokens:, :] += x_re * g_im + x_im * g_re
 
     absorb(send[me], me)
-    for s in order:
-        main_copies[s].wait_recv()
-        edge_copies[s].wait_recv()
+
+    @pl.loop(0, parts - 1)
+    def _(t):
+        s = turn(t)
+        main_copy(s).wait_recv()
+        edge_copy(s).wait_recv()
         absorb(recv[behind(s)], behind(s))
 
     def restore(m):
@@ -259,13 +292,14 @@
             inv_ref[...], prod[m], precision=HIGH, preferred_element_type=jnp.float32
         )
 
-    for s in order:
-        m = ahead(s)
-        conv[m] = restore(m)
-        copy = remote(conv.at[m], back.at[me], back_sems, s, m)
-        copy.start()
-        back_copies[s] = copy
-    conv[me] = restore(me)
+    @pl.loop(0, parts)
+    def _(t):
+        s = turn(t)
+        conv[ahead(s)] = restore(ahead(s))
+
+        @pl.when(t < parts - 1)
+        def _():
+            back_copy(s).start()
 
     def gate(result, d):
         q_short = jnp.concatenate(
@@ -277,16 +311,24 @@
         else:
             out_ref[d] = value
 
-    for s in order + [0]:
-        block_loads[0, s].wait()
+    @pl.loop(0, parts)
+    def _(t):
+        block_load(0, q_hbm, q_ref, turn(t)).wait()
+
     gate(conv[me], me)
-    for s in order:
-        back_copies[s].wait_recv()
+
+    @pl.loop(0, parts - 1)
+    def _(t):
+        s = turn(t)
+        back_copy(s).wait_recv()
         gate(back[behind(s)], behind(s))
-    for s in order:
-        main_copies[s].wait_send()
-        edge_copies[s].wait_send()
-        back_copies[s].wait_send()
+
+    @pl.loop(0, parts - 1)
+    def _(t):
+        s = turn(t)
+        main_copy(s).wait_send()
+        edge_copy(s).wait_send()
+        back_copy(s).wait_send()
 
 
 def local(
@@ -353,7 +395,7 @@
             sems, sems, sems,
         ],
         compiler_params=pltpu.CompilerParams(
-            collective_id=0, has_side_effects=True, vmem_limit_bytes=62 * 1024 * 1024
+            collective_id=0, has_side_effects=True, vmem_limit_bytes=59 * 1024 * 1024
         ),
         cost_estimate=pl.CostEstimate(
             flops=6 * length * tokens * cw * 8, bytes_accessed=16 * tokens * width,

time: 38.9 us -> 38.6 us (level)
  Pallas kernels: 36.9 us -> 36.5 us
where the time goes in v3:
time: 38.6 us; the launch traced here: 38.4 us
  Pallas kernels  36.5 us (95%)
  local copies, waits for them, and re-layouts  1.89 us (5%)
    pallas_call x1, Pallas kernels, local(): pl.pallas_call(functools.partial(kernel, parts, flat), out_shape=jax.Shap...  36.5 us
    unnamed x1, local copies, waits for them, and re-layouts  1.89 us

profile of v3, /device:TPU:0, one launch (start us, length us, event | category | flops | bytes accessed | tf_op | source)
XLA Modules:
  0.0 38.4 jit_solution(1905878445442234155)
XLA Ops:
  0.0 36.5 %shard_map.136 = f32[128,1024]{1,0:T(8,128)} custom-call(f32[128,1024]{1,0:T(8,128)} %q_hbm.1, f32[128,1024]{1,0:T(8,128)} %k_hbm.1, f32[128,1024]{1,0:T(8,128)} %v_hbm.1, f32[3,3,1024]{2,1,0:T(4,128)} %taps_hbm.1, s32[16]{0:T(128)} %freq_ref.1, f32[33,64]{1,0:T(8,128)} %w1_hbm.1, f32[1,64]{1,0:T(1,128)} %bitcast.6, f32[64,64]{1,0:T(8,128)} %w2_hbm.1, ...), custom_call_target="tpu_custom_call" | custom-call | flops 805306368 | bytes 2097152 | tf_op jit(solution)/shard_map/pallas_call | solution.py:365
  36.5 1.9 %copy.16 = f32[128,1024]{1,0:T(8,128)} copy(f32[128,1024]{1,0:T(8,128)} %shard_map.136) | data formatting | bytes 1048576

commit v4 on v3

--- a/solution.py
+++ b/solution.py
@@ -268,7 +268,7 @@
 
     def absorb(block, i):
         spec[...] = jnp.dot(
-            fwd_ref[:, 0:tokens], block, precision=HIGH, preferred_element_type=jnp.float32
+            fwd_ref[:, 0:tokens], block, precision=lax.Precision.HIGH, preferred_element_type=jnp.float32
         )
 
         @pl.loop(0, parts - i)
@@ -289,7 +289,7 @@
 
     def restore(m):
         return jnp.dot(
-            inv_ref[...], prod[m], precision=HIGH, preferred_element_type=jnp.float32
+            inv_ref[...], prod[m], precision=lax.Precision.HIGH, preferred_element_type=jnp.float32
         )
 
     @pl.loop(0, parts)

time: 38.6 us -> 38.2 us (0.990)
  Pallas kernels: 36.5 us -> 36.1 us
    pallas_call x1, Pallas kernels: 36.5 us -> 36.1 us  [local(): pl.pallas_call(functools.partial(kernel, parts, flat), out_shape=jax.Shap...]
where the time goes in v4:
time: 38.2 us; the launch traced here: 38 us
  Pallas kernels  36.1 us (95%)
  local copies, waits for them, and re-layouts  1.89 us (5%)
    pallas_call x1, Pallas kernels, local(): pl.pallas_call(functools.partial(kernel, parts, flat), out_shape=jax.Shap...  36.1 us
    unnamed x1, local copies, waits for them, and re-layouts  1.89 us

profile of v4, /device:TPU:0, one launch (start us, length us, event | category | flops | bytes accessed | tf_op | source)
XLA Modules:
  0.0 38.0 jit_solution(15926639000980093622)
XLA Ops:
  0.0 36.1 %shard_map.136 = f32[128,1024]{1,0:T(8,128)} custom-call(f32[128,1024]{1,0:T(8,128)} %q_hbm.1, f32[128,1024]{1,0:T(8,128)} %k_hbm.1, f32[128,1024]{1,0:T(8,128)} %v_hbm.1, f32[3,3,1024]{2,1,0:T(4,128)} %taps_hbm.1, s32[16]{0:T(128)} %freq_ref.1, f32[33,64]{1,0:T(8,128)} %w1_hbm.1, f32[1,64]{1,0:T(1,128)} %bitcast.6, f32[64,64]{1,0:T(8,128)} %w2_hbm.1, ...), custom_call_target="tpu_custom_call" | custom-call | flops 805306368 | bytes 2097152 | tf_op jit(solution)/shard_map/pallas_call | solution.py:365
  36.1 1.9 %copy.16 = f32[128,1024]{1,0:T(8,128)} copy(f32[128,1024]{1,0:T(8,128)} %shard_map.136) | data formatting | bytes 1048576
